TPU v7x, 32 devices: a whole 2x2x4 slice. The times are simulated.
32 devices in a mesh: group: 2 (over x), frame: 16 (over z, y, core).
Axes of the slice: x: 2, y: 2, z: 4, core: 2. Of those that a mesh axis runs over, the one named last changes fastest.
Arguments:
- queries: bfloat16 [10240, 5120], P(('group', 'frame')), parts along dimension 0, may hold values from -33 to 33
- keys: bfloat16 [10240, 5120], P(('group', 'frame')), parts along dimension 0, may hold values from -33 to 33
- values: bfloat16 [10240, 5120], P(('group', 'frame')), parts along dimension 0, may hold values from -6 to 6
- labels: int32 [80], P('group'), parts along dimension 0, may hold values from 0 to 1, as said below
- band: int32 [80], P('group'), parts along dimension 0, may hold values from 2 to 4
Outputs:
- attended: bfloat16 [10240, 5120], P(('group', 'frame')), parts along dimension 0
There are 2 independent parts, one for each index of `group`. A program takes and returns all parts, laid end to end along the dimension named above; each array names one. Nothing has to cross between parts.
Inputs may be any that keep to these rules, and one draw needn't show every extreme that they name: `labels`: exactly 10 of the 40 heads carry 1, the others 0.
All inputs are finite; a program needn't handle non-finite values.
Results may differ from a plain program's by a relative error of at most 0.0049.
Values may be sent and summed in bfloat16 or wider, within the bound.
A program may use at most 128 MiB of HBM per device.

v0:
```python
import math
import jax
import jax.numpy as jnp
from jax import lax
from jax.sharding import PartitionSpec as P

TEMP_HEADS = 10


def from_partner(block, axis, bit):
    count = lax.axis_size(axis)
    route = []
    for low in range(count):
        high = low | 1 << bit
        if high != low and high < count:
            route += [(low, high), (high, low)]
    return lax.ppermute(block, axis, route)


def softmax_rounded(scores):
    peak = jnp.max(scores, axis=-1, keepdims=True)
    weights = jnp.exp(scores - peak)
    return (weights / jnp.sum(weights, axis=-1, keepdims=True)).astype(jnp.bfloat16)


def block_heads(count):
    for candidate in (6, 5, 4, 3, 2):
        if count % candidate == 0:
            return candidate
    return 1


def attend_spatial(query_part, key_all, value_all):
    head_total = query_part.shape[1]
    step_heads = block_heads(head_total)
    scale = 1.0 / math.sqrt(query_part.shape[2])

    def one_block(block_number, result):
        start = block_number * step_heads
        query_block = lax.dynamic_slice_in_dim(query_part, start, step_heads, 1)
        key_block = lax.dynamic_slice_in_dim(key_all, start, step_heads, 1)
        value_block = lax.dynamic_slice_in_dim(value_all, start, step_heads, 1)
        scores = (
            jnp.einsum("rhd,khd->hrk", query_block, key_block, preferred_element_type=jnp.float32)
            * scale
        )
        weights = softmax_rounded(scores)
        output_block = jnp.einsum(
            "hrk,khd->rhd", weights, value_block, preferred_element_type=jnp.float32
        ).astype(jnp.bfloat16)
        return lax.dynamic_update_slice_in_dim(result, output_block, start, 1)

    initial = jnp.zeros(query_part.shape, jnp.bfloat16)
    return lax.fori_loop(0, head_total // step_heads, one_block, initial)


def attend_columns(query_part, key_part, value_part, head_band):
    query_cols, key_cols, value_cols = (
        lax.all_to_all(query_part[None], "frame", split_axis=1, concat_axis=0, tiled=True),
        lax.all_to_all(key_part[None], "frame", split_axis=1, concat_axis=0, tiled=True),
        lax.all_to_all(value_part[None], "frame", split_axis=1, concat_axis=0, tiled=True),
    )
    sources, pixels, head_part, head_size = query_cols.shape
    frames = sources // 2
    scale = 1.0 / math.sqrt(head_size)
    grid_shape = (frames, 2, pixels, head_part, head_size)
    scores = (
        jnp.einsum(
            "fapnd,gapnd->apnfg",
            query_cols.reshape(grid_shape),
            key_cols.reshape(grid_shape),
            preferred_element_type=jnp.float32,
        )
        * scale
    )
    frame_ids = jnp.arange(frames, dtype=jnp.int32)
    distance = jnp.abs(frame_ids[:, None] - frame_ids[None, :])
    keep = distance[None, :, :] <= head_band[:, None, None]
    scores = jnp.where(keep, scores, jnp.float32(-1e30))
    weights = softmax_rounded(scores)
    output = jnp.einsum(
        "apnfg,gapnd->fapnd",
        weights,
        value_cols.reshape(grid_shape),
        preferred_element_type=jnp.float32,
    ).astype(jnp.bfloat16)
    output = output.reshape(sources, pixels, head_part, head_size)
    returned = lax.all_to_all(output, "frame", split_axis=0, concat_axis=1, tiled=True)
    return returned[0]


def shards(queries, keys, values, labels, band):
    row_count = queries.shape[0]
    head_count = labels.shape[0]
    head_size = queries.shape[1] // head_count
    query_heads = queries.reshape(row_count, head_count, head_size)
    key_heads = keys.reshape(row_count, head_count, head_size)
    value_heads = values.reshape(row_count, head_count, head_size)
    spatial_count = head_count - TEMP_HEADS
    ordering = jnp.argsort(labels, stable=True)
    spatial_index = ordering[:spatial_count]
    temporal_index = ordering[spatial_count:]
    inverse = jnp.argsort(ordering, stable=True)
    query_spatial = jnp.take(query_heads, spatial_index, axis=1)
    key_spatial = jnp.take(key_heads, spatial_index, axis=1)
    value_spatial = jnp.take(value_heads, spatial_index, axis=1)
    temporal_band = jnp.take(band, temporal_index)
    temporal = attend_columns(
        jnp.take(query_heads, temporal_index, axis=1),
        jnp.take(key_heads, temporal_index, axis=1),
        jnp.take(value_heads, temporal_index, axis=1),
        temporal_band,
    )
    parity = lax.axis_index("frame") % 2
    half = spatial_count // 2
    mine_start = parity * half
    other_start = (1 - parity) * half
    query_mine = lax.dynamic_slice_in_dim(query_spatial, mine_start, half, 1)
    key_mine = lax.dynamic_slice_in_dim(key_spatial, mine_start, half, 1)
    value_mine = lax.dynamic_slice_in_dim(value_spatial, mine_start, half, 1)
    query_other = lax.dynamic_slice_in_dim(query_spatial, other_start, half, 1)
    key_other = lax.dynamic_slice_in_dim(key_spatial, other_start, half, 1)
    value_other = lax.dynamic_slice_in_dim(value_spatial, other_start, half, 1)
    query_got, key_got, value_got = from_partner((query_other, key_other, value_other), "frame", 0)

    def whole_frame(own, got):
        return jnp.where(
            parity == 0, jnp.concatenate([own, got], axis=0), jnp.concatenate([got, own], axis=0)
        )

    frame_out = attend_spatial(
        whole_frame(query_mine, query_got),
        whole_frame(key_mine, key_got),
        whole_frame(value_mine, value_got),
    )
    own_rows = lax.dynamic_slice_in_dim(frame_out, parity * row_count, row_count, 0)
    other_rows = lax.dynamic_slice_in_dim(frame_out, (1 - parity) * row_count, row_count, 0)
    returned = from_partner(other_rows, "frame", 0)
    spatial = jnp.where(
        parity == 0,
        jnp.concatenate([own_rows, returned], axis=1),
        jnp.concatenate([returned, own_rows], axis=1),
    )
    combined = jnp.take(jnp.concatenate([spatial, temporal], axis=1), inverse, axis=1)
    return combined.reshape(row_count, head_count * head_size)


def solution(mesh):
    placed = (
        P(("group", "frame"), None),
        P(("group", "frame"), None),
        P(("group", "frame"), None),
        P("group"),
        P("group"),
    )
    return jax.shard_map(
        shards, mesh=mesh, in_specs=placed, out_specs=P(("group", "frame"), None), check_vma=False
    )
```

profile of v0, /device:TPU:9, one launch (start us, length us, event | category | flops | bytes accessed | tf_op | source)
XLA Modules:
  0.0 212.5 jit_solution(6797831736654225508)
XLA Ops:
  6.7 4.7 %copy_bitcast_fusion = bf16[320,40,128]{2,0,1:T(8,128)(2,1)} fusion(bf16[320,5120]{1,0:T(8,128)(2,1)} %param.12), kind=kLoop, calls=%fused_computation.29 | loop fusion | bytes 6553600 | tf_op jit(solution)/shard_map/reshape | solution.py:97
  13.0 3.5 %gather_fusion.7 = bf16[10,320,128]{2,1,0:T(8,128)(2,1)} fusion(bf16[320,40,128]{2,0,1:T(8,128)(2,1)} %copy_bitcast_fusion, s32[1024]{0:T(1024)S(1)} %pad_clamp_fusion.1), kind=kCustom, calls=%fused_computation.5.clone | custom fusion | bytes 1638440 | tf_op jit(solution)/shard_map/jit(_take)/gather | solution.py:110
  16.5 4.5 %copy_bitcast_fusion.2 = bf16[320,40,128]{2,0,1:T(8,128)(2,1)} fusion(bf16[320,5120]{1,0:T(8,128)(2,1)} %param.13), kind=kLoop, calls=%fused_computation.31 | loop fusion | bytes 6553600 | tf_op jit(solution)/shard_map/reshape | solution.py:98
  21.0 3.5 %gather_fusion.5 = bf16[10,320,128]{2,1,0:T(8,128)(2,1)} fusion(bf16[320,40,128]{2,0,1:T(8,128)(2,1)} %copy_bitcast_fusion.2, s32[1024]{0:T(1024)S(1)} %pad_clamp_fusion.1), kind=kCustom, calls=%fused_computation.1.clone | custom fusion | bytes 1638440 | tf_op jit(solution)/shard_map/jit(_take)/gather | solution.py:111
  29.4 6.6 %all-to-all-start.2 = ((bf16[1,320,10,128]{3,2,0,1:T(8,128)(2,1)}), bf16[1,320,10,128]{3,2,0,1:T(8,128)(2,1)}, u32[]{:S(2)}, u32[]{:S(2)}) async-start(bf16[1,320,10,128]{3,2,0,1:T(8,128)(2,1)} %copy.97), calls=%async_computation.2 | async-start | bytes 2621440 | tf_op jit(solution)/shard_map/all_to_all | solution.py:60
  36.1 4.3 %gather_fusion.4 = bf16[30,320,128]{2,1,0:T(8,128)(2,1)} fusion(bf16[320,40,128]{2,0,1:T(8,128)(2,1)} %copy_bitcast_fusion, s32[1024]{0:T(1024)S(1)} %pad_clamp_fusion.2), kind=kCustom, calls=%fused_computation.3.clone | custom fusion | bytes 4915320 | tf_op jit(solution)/shard_map/jit(_take)/gather | solution.py:105
  42.7 4.4 %gather_fusion.2 = bf16[30,320,128]{2,1,0:T(8,128)(2,1)} fusion(bf16[320,40,128]{2,0,1:T(8,128)(2,1)} %copy_bitcast_fusion.2, s32[1024]{0:T(1024)S(1)} %pad_clamp_fusion.2), kind=kCustom, calls=%fused_computation.clone | custom fusion | bytes 4915320 | tf_op jit(solution)/shard_map/jit(_take)/gather | solution.py:106
  47.1 4.6 %select_bitcast_fusion = (bf16[320,30,128]{2,0,1:T(8,128)(2,1)}, bf16[320,30,128]{2,0,1:T(8,128)(2,1)S(1)}, bf16[320,30,128]{2,0,1:T(8,128)(2,1)S(1)}) fusion(bf16[30,320,128]{2,1,0:T(8,128)(2,1)S(1)} %copy-done.5, pred[30]{0:T(512)(128)(4,1)S(1)} %get-tuple-element.146, bf16[30,320,128]{2,1,0:T(8,128)(2,1)} %gather_fusion.3, ...), kind=kLoop, calls=%fused_computation.37 | loop fusion | flops 3686400 | bytes 14745630 | tf_op jit(solution)/shard_map/jit(_take)/select_n | solution.py:105
  57.1 9.3 %all-to-all-done.2 = bf16[1,320,10,128]{3,2,0,1:T(8,128)(2,1)} async-done(((bf16[1,320,10,128]{3,2,0,1:T(8,128)(2,1)}), bf16[1,320,10,128]{3,2,0,1:T(8,128)(2,1)}, u32[]{:S(2)}, u32[]{:S(2)}) %all-to-all-start.2) | async-done | bytes 819232 | tf_op jit(solution)/shard_map/all_to_all | solution.py:60
  66.3 5.2 %all-to-all-start.1 = ((bf16[1,320,10,128]{3,2,0,1:T(8,128)(2,1)}), bf16[1,320,10,128]{3,2,0,1:T(8,128)(2,1)}, u32[]{:S(2)}, u32[]{:S(2)}) async-start(bf16[1,320,10,128]{3,2,0,1:T(8,128)(2,1)} %copy.94), calls=%async_computation.1 | async-start | bytes 2621440 | tf_op jit(solution)/shard_map/all_to_all | solution.py:59
  77.2 4.0 %maximum_select_fusion = bf16[640,15,128]{2,0,1:T(8,128)(2,1)} fusion(bf16[320,15,128]{2,0,1:T(8,128)(2,1)} %collective-permute-done, bf16[320,15,128]{2,0,1:T(8,128)(2,1)S(1)} %copy-done.8, pred[]{:T(512)S(6)} %eq.4), kind=kLoop, calls=%fused_computation.33 | loop fusion | flops 11059200 | bytes 4915201 | tf_op jit(solution)/shard_map/jit(_where)/select_n | solution.py:127
  81.2 4.0 %maximum_select_fusion.1 = bf16[640,15,128]{2,0,1:T(8,128)(2,1)} fusion(bf16[320,15,128]{2,0,1:T(8,128)(2,1)} %collective-permute-done.1, bf16[320,15,128]{2,0,1:T(8,128)(2,1)S(1)} %copy-done.9, pred[]{:T(512)S(6)} %eq.4), kind=kLoop, calls=%fused_computation.34 | loop fusion | flops 11059200 | bytes 4915201 | tf_op jit(solution)/shard_map/jit(_where)/select_n | solution.py:127
  85.2 3.8 %maximum_select_fusion.2 = bf16[640,15,128]{2,0,1:T(8,128)(2,1)} fusion(bf16[320,15,128]{2,0,1:T(8,128)(2,1)} %collective-permute-done.2, bf16[320,15,128]{2,0,1:T(8,128)(2,1)S(1)} %copy-done.10, pred[]{:T(512)S(6)} %eq.4), kind=kLoop, calls=%fused_computation.35 | loop fusion | flops 11059200 | bytes 4915201 | tf_op jit(solution)/shard_map/jit(_where)/select_n | solution.py:127
  89.0 12.9 %all-to-all-done.1 = bf16[1,320,10,128]{3,2,0,1:T(8,128)(2,1)} async-done(((bf16[1,320,10,128]{3,2,0,1:T(8,128)(2,1)}), bf16[1,320,10,128]{3,2,0,1:T(8,128)(2,1)}, u32[]{:S(2)}, u32[]{:S(2)}) %all-to-all-start.1) | async-done | bytes 819232 | tf_op jit(solution)/shard_map/all_to_all | solution.py:59
  101.9 5.3 %all-to-all-start = ((bf16[1,320,10,128]{3,2,0,1:T(8,128)(2,1)}), bf16[1,320,10,128]{3,2,0,1:T(8,128)(2,1)S(1)}, u32[]{:S(2)}, u32[]{:S(2)}) async-start(bf16[1,320,10,128]{3,2,0,1:T(8,128)(2,1)} %copy.91), calls=%async_computation | async-start | bytes 2621440 | tf_op jit(solution)/shard_map/all_to_all | solution.py:61
  109.0 50.4 %while.13 = (s32[]{:T(128)}, bf16[640,15,128]{2,0,1:T(8,128)(2,1)}, bf16[640,15,128]{2,0,1:T(8,128)(2,1)}, bf16[640,15,128]{2,0,1:T(8,128)(2,1)}, bf16[640,15,12...) while((s32[]{:T(128)}, bf16[640,15,128]{2,0,1:T(8,128)(2,1)}, ...), condition=%wide.region_5.7_spmd, body=%wide.region_2.6_spmd.sunk | while | flops 1067422080 | bytes 72116400 | solution.py:54
  114.8 8.7 %fusion.50 = bf16[640,5,128]{0,2,1:T(8,128)(2,1)S(1)} fusion(f32[5,640]{1,0:T(8,128)S(1)} %fusion.49, bf16[640,15,128]{2,0,1:T(8,128)(2,1)} %get-tuple-element.217, s32[]{:T(128)S(6)} %select_n.164, f32[5,640,640]{1,2,0:T(8,128)} %copy-done.3), kind=kOutput, calls=%fused_computation.16.clone.1 | convolution fusion | flops 534941440 | bytes 18035204 | tf_op jit(solution)/shard_map/while/body/eval_jaxpr/hrk,khd->rhd/dot_general | solution.py:48
  131.6 8.7 %fusion.50 = bf16[640,5,128]{0,2,1:T(8,128)(2,1)S(1)} fusion(f32[5,640]{1,0:T(8,128)S(1)} %fusion.49, bf16[640,15,128]{2,0,1:T(8,128)(2,1)} %get-tuple-element.217, s32[]{:T(128)S(6)} %select_n.164, f32[5,640,640]{1,2,0:T(8,128)} %copy-done.3), kind=kOutput, calls=%fused_computation.16.clone.1 | convolution fusion | flops 534941440 | bytes 18035204 | tf_op jit(solution)/shard_map/while/body/eval_jaxpr/hrk,khd->rhd/dot_general | solution.py:48
  148.4 8.7 %fusion.50 = bf16[640,5,128]{0,2,1:T(8,128)(2,1)S(1)} fusion(f32[5,640]{1,0:T(8,128)S(1)} %fusion.49, bf16[640,15,128]{2,0,1:T(8,128)(2,1)} %get-tuple-element.217, s32[]{:T(128)S(6)} %select_n.164, f32[5,640,640]{1,2,0:T(8,128)} %copy-done.3), kind=kOutput, calls=%fused_computation.16.clone.1 | convolution fusion | flops 534941440 | bytes 18035204 | tf_op jit(solution)/shard_map/while/body/eval_jaxpr/hrk,khd->rhd/dot_general | solution.py:48
  159.4 4.2 %exponential_reduce_fusion = (f32[2,20,10,8]{3,2,1,0:T(8,128)}, f32[2,20,10,8,8]{3,4,2,1,0:T(8,128)S(1)}) fusion(bf16[8,2,20,10,128]{4,3,2,1,0:T(8,128)(2,1)} %bitcast.13, bf16[8,2,20,10,128]{4,3,2,1,0:T(8,128)(2,1)} %bitcast.10, pred[10,8,8]{1,2,0:T(8,128)(4,1)S(1)} %broadcast_compare_fusion), kind=kOutput, calls=%fused_computation.43 | convolution fusion | flops 6656007 | bytes 1754240 | tf_op jit(solution)/shard_map/sub | solution.py:22
  168.0 6.0 %all-to-all-start.3 = ((bf16[16,20,10,128]{3,1,2,0:T(8,128)(2,1)}), bf16[16,20,10,128]{3,1,2,0:T(8,128)(2,1)}, u32[]{:S(2)}, u32[]{:S(2)}) async-start(bf16[16,20,10,128]{3,1,2,0:T(8,128)(2,1)} %copy.104), calls=%async_computation.3 | async-start | bytes 1966080 | tf_op jit(solution)/shard_map/all_to_all | solution.py:88
  182.6 15.1 %all-to-all-done.3 = bf16[16,20,10,128]{3,1,2,0:T(8,128)(2,1)} async-done(((bf16[16,20,10,128]{3,1,2,0:T(8,128)(2,1)}), bf16[16,20,10,128]{3,1,2,0:T(8,128)(2,1)}, u32[]{:S(2)}, u32[]{:S(2)}) %all-to-all-start.3) | async-done | bytes 819232 | tf_op jit(solution)/shard_map/all_to_all | solution.py:88
  203.3 4.9 %gather_fusion.1 = bf16[40,320,128]{2,1,0:T(8,128)(2,1)} fusion(bf16[320,40,128]{2,0,1:T(8,128)(2,1)} %pad_maximum_fusion, s32[1024]{0:T(1024)S(1)} %pad_clamp_fusion), kind=kCustom, calls=%fused_computation.7 | custom fusion | bytes 6553760 | tf_op jit(solution)/shard_map/jit(_take)/gather | solution.py:144
  208.2 4.3 %bitcast_select_fusion = bf16[320,5120]{1,0:T(8,128)(2,1)} fusion(pred[5120]{0:T(1024)(128)(4,1)S(1)} %broadcast_bitcast_fusion, bf16[40,320,128]{2,1,0:T(8,128)(2,1)} %gather_fusion.1), kind=kLoop, calls=%fused_computation.28 | loop fusion | flops 1638400 | bytes 6558720 | tf_op jit(solution)/shard_map/jit(_take)/select_n | solution.py:144
  (88 shorter events, 71.3 us)
Async XLA Ops:
  0.0 1.9 copy-start
  0.0 4.5 %copy-start.13 = (s32[40]{0:T(128)S(1)}, s32[40]{0:T(128)}, u32[]{:S(2)}) copy-start(s32[40]{0:T(128)} %param.14) | copy-start | bytes 484
  6.7 4.7 %copy-start.4 = (bf16[320,40,128]{2,0,1:T(8,128)(2,1)S(1)}, bf16[320,40,128]{2,0,1:T(8,128)(2,1)}, u32[]{:S(2)}) copy-start(bf16[320,40,128]{2,0,1:T(8,128)(2,1)} %copy_bitcast_fusion.1) | copy-start | bytes 9830404
  29.4 36.9 %all-to-all-start.2 = ((bf16[1,320,10,128]{3,2,0,1:T(8,128)(2,1)}), bf16[1,320,10,128]{3,2,0,1:T(8,128)(2,1)}, u32[]{:S(2)}, u32[]{:S(2)}) async-start(bf16[1,320,10,128]{3,2,0,1:T(8,128)(2,1)} %copy.97), calls=%async_computation.2 | async-start | bytes 2621440 | tf_op jit(solution)/shard_map/all_to_all | solution.py:60
  42.7 4.4 %copy-start.5 = (bf16[30,320,128]{2,1,0:T(8,128)(2,1)S(1)}, bf16[30,320,128]{2,1,0:T(8,128)(2,1)}, u32[]{:S(2)}) copy-start(bf16[30,320,128]{2,1,0:T(8,128)(2,1)} %gather_fusion.4) | copy-start | bytes 7372804
  53.3 23.9 %collective-permute-start = (bf16[320,15,128]{2,0,1:T(8,128)(2,1)}, bf16[320,15,128]{2,0,1:T(8,128)(2,1)}, u32[]{:S(2)}, u32[]{:S(2)}) collective-permute-start(bf16[320,15,128]{2,0,1:T(8,128)(2,1)} %get-tuple-element.157), channel_id=1, source_target_pairs={{0,1},{1,0},{2,3},{3,2},{4,5},{5,4},{6,7},{7,6},{8,9},{9,8},{10,11... | collective-permute-start | bytes 3686408 | tf_op jit(solution)/shard_map/ppermute | solution.py:17
  53.6 1.8 copy-start.11
  55.3 16.3 %copy-start.6 = (bf16[320,30,128]{2,0,1:T(8,128)(2,1)S(1)}, bf16[320,30,128]{2,0,1:T(8,128)(2,1)}, u32[]{:S(2)}) copy-start(bf16[320,30,128]{2,0,1:T(8,128)(2,1)} %get-tuple-element.158) | copy-start | bytes 7372804
  55.3 26.0 %collective-permute-start.1 = (bf16[320,15,128]{2,0,1:T(8,128)(2,1)}, bf16[320,15,128]{2,0,1:T(8,128)(2,1)}, u32[]{:S(2)}, u32[]{:S(2)}) collective-permute-start(bf16[320,15,128]{2,0,1:T(8,128)(2,1)} %get-tuple-element.155), channel_id=1, source_target_pairs={{0,1},{1,0},{2,3},{3,2},{4,5},{5,4},{6,7},{7,6},{8,9},{9,8},{10,11... | collective-permute-start | bytes 3686408 | tf_op jit(solution)/shard_map/ppermute | solution.py:17
  66.3 35.5 %all-to-all-start.1 = ((bf16[1,320,10,128]{3,2,0,1:T(8,128)(2,1)}), bf16[1,320,10,128]{3,2,0,1:T(8,128)(2,1)}, u32[]{:S(2)}, u32[]{:S(2)}) async-start(bf16[1,320,10,128]{3,2,0,1:T(8,128)(2,1)} %copy.94), calls=%async_computation.1 | async-start | bytes 2621440 | tf_op jit(solution)/shard_map/all_to_all | solution.py:59
  71.6 4.8 %copy-start.2 = (s32[40]{0:T(128)S(1)}, s32[40]{0:T(128)}, u32[]{:S(2)}) copy-start(s32[40]{0:T(128)} %param.15) | copy-start | bytes 484
  73.2 4.0 %copy-start.8 = (bf16[320,15,128]{2,0,1:T(8,128)(2,1)S(1)}, bf16[320,15,128]{2,0,1:T(8,128)(2,1)}, u32[]{:S(2)}) copy-start(bf16[320,15,128]{2,0,1:T(8,128)(2,1)} %get-tuple-element.156) | copy-start | bytes 3686404
  73.2 11.9 %collective-permute-start.2 = (bf16[320,15,128]{2,0,1:T(8,128)(2,1)}, bf16[320,15,128]{2,0,1:T(8,128)(2,1)}, u32[]{:S(2)}, u32[]{:S(2)}) collective-permute-start(bf16[320,15,128]{2,0,1:T(8,128)(2,1)} %get-tuple-element.153), channel_id=1, source_target_pairs={{0,1},{1,0},{2,3},{3,2},{4,5},{5,4},{6,7},{7,6},{8,9},{9,8},{10,11... | collective-permute-start | bytes 3686408 | tf_op jit(solution)/shard_map/ppermute | solution.py:17
  77.2 4.0 %copy-start.9 = (bf16[320,15,128]{2,0,1:T(8,128)(2,1)S(1)}, bf16[320,15,128]{2,0,1:T(8,128)(2,1)}, u32[]{:S(2)}) copy-start(bf16[320,15,128]{2,0,1:T(8,128)(2,1)} %get-tuple-element.154) | copy-start | bytes 3686404
  81.2 4.0 %copy-start.10 = (bf16[320,15,128]{2,0,1:T(8,128)(2,1)S(1)}, bf16[320,15,128]{2,0,1:T(8,128)(2,1)}, u32[]{:S(2)}) copy-start(bf16[320,15,128]{2,0,1:T(8,128)(2,1)} %get-tuple-element.152) | copy-start | bytes 3686404
  101.9 61.8 %all-to-all-start = ((bf16[1,320,10,128]{3,2,0,1:T(8,128)(2,1)}), bf16[1,320,10,128]{3,2,0,1:T(8,128)(2,1)S(1)}, u32[]{:S(2)}, u32[]{:S(2)}) async-start(bf16[1,320,10,128]{3,2,0,1:T(8,128)(2,1)} %copy.91), calls=%async_computation | async-start | bytes 2621440 | tf_op jit(solution)/shard_map/all_to_all | solution.py:61
  111.7 3.2 %copy-start.3 = (f32[5,640,640]{1,2,0:T(8,128)}, f32[5,640,640]{1,2,0:T(8,128)S(1)}, u32[]{:S(2)}) copy-start(f32[5,640,640]{1,2,0:T(8,128)S(1)} %fusion.48) | copy-start | bytes 24576004 | tf_op jit(solution)/shard_map/while
  128.4 3.2 %copy-start.3 = (f32[5,640,640]{1,2,0:T(8,128)}, f32[5,640,640]{1,2,0:T(8,128)S(1)}, u32[]{:S(2)}) copy-start(f32[5,640,640]{1,2,0:T(8,128)S(1)} %fusion.48) | copy-start | bytes 24576004 | tf_op jit(solution)/shard_map/while
  145.2 3.2 %copy-start.3 = (f32[5,640,640]{1,2,0:T(8,128)}, f32[5,640,640]{1,2,0:T(8,128)S(1)}, u32[]{:S(2)}) copy-start(f32[5,640,640]{1,2,0:T(8,128)S(1)} %fusion.48) | copy-start | bytes 24576004 | tf_op jit(solution)/shard_map/while
  165.5 8.6 %copy-start.7 = (bf16[640,15,128]{2,0,1:T(8,128)(2,1)S(1)}, bf16[640,15,128]{2,0,1:T(8,128)(2,1)}, u32[]{:S(2)}) copy-start(bf16[640,15,128]{2,0,1:T(8,128)(2,1)} %get-tuple-element.105) | copy-start | bytes 7372804
  168.0 29.6 %all-to-all-start.3 = ((bf16[16,20,10,128]{3,1,2,0:T(8,128)(2,1)}), bf16[16,20,10,128]{3,1,2,0:T(8,128)(2,1)}, u32[]{:S(2)}, u32[]{:S(2)}) async-start(bf16[16,20,10,128]{3,1,2,0:T(8,128)(2,1)} %copy.104), calls=%async_computation.3 | async-start | bytes 1966080 | tf_op jit(solution)/shard_map/all_to_all | solution.py:88
  175.7 3.1 %collective-permute-start.3 = (bf16[320,15,128]{2,0,1:T(8,128)(2,1)}, bf16[320,15,128]{2,0,1:T(8,128)(2,1)S(1)}, u32[]{:S(2)}, u32[]{:S(2)}) collective-permute-start(bf16[320,15,128]{2,0,1:T(8,128)(2,1)} %get-tuple-element.151), channel_id=1, source_target_pairs={{0,1},{1,0},{2,3},{3,2},{4,5},{5,4},{6,7},{7,6},{8,9},{9,8},{10,11... | collective-permute-start | bytes 3686408 | tf_op jit(solution)/shard_map/ppermute | solution.py:17
  178.8 1.0 copy-start.12
  203.3 9.2 %copy-start.1 = (bf16[320,5120]{1,0:T(8,128)(2,1)S(1)}, bf16[320,5120]{1,0:T(8,128)(2,1)}, u32[]{:S(2)}) copy-start(bf16[320,5120]{1,0:T(8,128)(2,1)} %param.11) | copy-start | bytes 9830404
where the time goes:
time: 213 us
  local copies, waits for them, and re-layouts  71.1 us (33%)
  matrix products  39.9 us (19%)
  other arithmetic  39.1 us (18%)
  waiting for transfers between devices  37.8 us (18%)
  starting transfers between devices  24.4 us (11%)
    dot_general x3, matrix products, one_block(): jnp.einsum('hrk,khd->rhd', weights, value_block, preferred_element_type=j...  26 us
    all_to_all x1, waiting for transfers between devices, attend_columns(): lax.all_to_all(output, 'frame', split_axis=0, concat_axis=1, tiled=True)  15.1 us
    all_to_all x1, waiting for transfers between devices, attend_columns(): lax.all_to_all(query_part[None], 'frame', split_axis=1, concat_axis=0, ti...  12.9 us
    select_n x3, other arithmetic, whole_frame(): jnp.where(parity == 0, jnp.concatenate([own, got], axis=0), jnp.concatena...  11.7 us
    all_to_all x1, waiting for transfers between devices, attend_columns(): lax.all_to_all(key_part[None], 'frame', split_axis=1, concat_axis=0, tile...  9.25 us
    dot_general x3, matrix products, one_block(): jnp.einsum('rhd,khd->hrk', query_block, key_block, preferred_element_type...  7.85 us
    dynamic_update_slice x6, local copies, waits for them, and re-layouts, one_block(): return lax.dynamic_update_slice_in_dim(result, output_block, start, 1)  7.02 us
    all_to_all x1, starting transfers between devices, attend_columns(): lax.all_to_all(key_part[None], 'frame', split_axis=1, concat_axis=0, tile...  6.61 us
  transfers between devices with their start and end apart: 8, of which 4 were waited for; matrix products, arithmetic and copies ran while one was open for 46% of the time, Pallas kernels for 0%

commit v1 on v0

--- a/solution.py
+++ b/solution.py
@@ -56,7 +56,15 @@
 
 def attend_columns(query_part, key_part, value_part, head_band):
     query_cols, key_cols, value_cols = (
-        lax.all_to_all(query_part[None], "frame", split_axis=1, concat_axis=0, tiled=True),
+        jnp.concatenate(
+            lax.all_to_all(
+                jnp.stack(jnp.split(query_part[None], lax.axis_size("frame"), axis=1)),
+                "frame",
+                0,
+                0,
+            ),
+            axis=0,
+        ),
         lax.all_to_all(key_part[None], "frame", split_axis=1, concat_axis=0, tiled=True),
         lax.all_to_all(value_part[None], "frame", split_axis=1, concat_axis=0, tiled=True),
     )

time: 213 us -> 203 us (0.953)
  waiting for transfers between devices: 37.8 us -> 22.6 us
  local copies, waits for them, and re-layouts: 71.1 us -> 75.7 us
    all_to_all x1, waiting for transfers between devices: 9.25 us -> 0.71 us  [attend_columns(): lax.all_to_all(key_part[None], 'frame', split_axis=1, concat_axis=0, tile...]
    unnamed x26 -> x41, local copies, waits for them, and re-layouts: 3.02 us -> 10.7 us
    all_to_all x1, waiting for transfers between devices: 12.9 us -> 6.21 us  [attend_columns(): lax.all_to_all(jnp.stack(jnp.split(query_part[None], lax.axis_size('frame...]
  transfers between devices with their start and end apart: 8 -> 8, of which waited for: 4 -> 4; matrix products, arithmetic and copies ran while one was open for 46% -> 52% of each run, Pallas kernels for 0% -> 0%
where the time goes in v1:
time: 203 us; the launch traced here: 202 us
  local copies, waits for them, and re-layouts  75.7 us (37%)
  other arithmetic  39.9 us (20%)
  matrix products  39.7 us (20%)
  starting transfers between devices  24.1 us (12%)
  waiting for transfers between devices  22.6 us (11%)
    dot_general x3, matrix products, one_block(): jnp.einsum('hrk,khd->rhd', weights, value_block, preferred_element_type=j...  26 us
    all_to_all x1, waiting for transfers between devices, attend_columns(): lax.all_to_all(output, 'frame', split_axis=0, concat_axis=1, tiled=True)  15.1 us
    select_n x3, other arithmetic, whole_frame(): jnp.where(parity == 0, jnp.concatenate([own, got], axis=0), jnp.concatena...  11.7 us
    unnamed x41, local copies, waits for them, and re-layouts  10.7 us
    dot_general x3, matrix products, one_block(): jnp.einsum('rhd,khd->hrk', query_block, key_block, preferred_element_type...  7.85 us
    dynamic_update_slice x6, local copies, waits for them, and re-layouts, one_block(): return lax.dynamic_update_slice_in_dim(result, output_block, start, 1)  7.02 us
    all_to_all x1, starting transfers between devices, attend_columns(): lax.all_to_all(key_part[None], 'frame', split_axis=1, concat_axis=0, tile...  6.61 us
    sub x3, other arithmetic, softmax_rounded(): weights = jnp.exp(scores - peak)  6.35 us
  transfers between devices with their start and end apart: 8, of which 4 were waited for; matrix products, arithmetic and copies ran while one was open for 52% of the time, Pallas kernels for 0%

profile of v1, /device:TPU:9, one launch (start us, length us, event | category | flops | bytes accessed | tf_op | source)
XLA Modules:
  0.0 202.3 jit_solution(3691809183805339185)
XLA Ops:
  9.8 3.5 %gather_fusion.7 = bf16[10,320,128]{2,1,0:T(8,128)(2,1)} fusion(bf16[320,40,128]{2,0,1:T(8,128)(2,1)} %copy_bitcast_fusion, s32[1024]{0:T(1024)S(1)} %get-tuple-element.166), kind=kCustom, calls=%fused_computation.5.clone | custom fusion | bytes 1638440 | tf_op jit(solution)/shard_map/jit(_take)/gather | solution.py:118
  13.3 4.5 %copy_bitcast_fusion.2 = bf16[320,40,128]{2,0,1:T(8,128)(2,1)} fusion(bf16[320,5120]{1,0:T(8,128)(2,1)} %param.13), kind=kLoop, calls=%fused_computation.31 | loop fusion | bytes 6553600 | tf_op jit(solution)/shard_map/reshape | solution.py:106
  17.9 3.5 %gather_fusion.5 = bf16[10,320,128]{2,1,0:T(8,128)(2,1)} fusion(bf16[320,40,128]{2,0,1:T(8,128)(2,1)} %copy_bitcast_fusion.2, s32[1024]{0:T(1024)S(1)} %get-tuple-element.166), kind=kCustom, calls=%fused_computation.1.clone | custom fusion | bytes 1638440 | tf_op jit(solution)/shard_map/jit(_take)/gather | solution.py:119
  21.4 3.1 %select_bitcast_fusion.4 = (bf16[1,320,10,128]{3,1,2,0:T(8,128)(2,1)}, bf16[1,320,10,128]{3,1,2,0:T(8,128)(2,1)S(1)}, bf16[1,320,10,128]{3,1,2,0:T(8,128)(2,1)}) fusion(bf16[10,320,128]{2,1,0:T(8,128)(2,1)} %gather_fusion.6, pred[10]{0:T(512)(128)(4,1)S(1)} %get-tuple-element.148, bf16[10,320,128]{2,1,0:T(8,128)(2,1)} %gather_fusion.7, ...), kind=kLoop, calls=%fused_computation.50 | loop fusion | flops 1228800 | bytes 4915210 | tf_op jit(solution)/shard_map/broadcast_in_dim | solution.py:61
  26.3 6.6 %all-to-all-start.2 = ((bf16[1,320,10,128]{3,2,0,1:T(8,128)(2,1)}), bf16[1,320,10,128]{3,2,0,1:T(8,128)(2,1)}, u32[]{:S(2)}, u32[]{:S(2)}) async-start(bf16[1,320,10,128]{3,2,0,1:T(8,128)(2,1)} %copy.96), calls=%async_computation.2 | async-start | bytes 2621440 | tf_op jit(solution)/shard_map/all_to_all | solution.py:68
  32.9 4.3 %gather_fusion.4 = bf16[30,320,128]{2,1,0:T(8,128)(2,1)} fusion(bf16[320,40,128]{2,0,1:T(8,128)(2,1)} %copy_bitcast_fusion, s32[1024]{0:T(1024)S(1)} %get-tuple-element.167), kind=kCustom, calls=%fused_computation.3.clone | custom fusion | bytes 4915320 | tf_op jit(solution)/shard_map/jit(_take)/gather | solution.py:113
  39.5 4.4 %gather_fusion.2 = bf16[30,320,128]{2,1,0:T(8,128)(2,1)} fusion(bf16[320,40,128]{2,0,1:T(8,128)(2,1)} %copy_bitcast_fusion.2, s32[1024]{0:T(1024)S(1)} %get-tuple-element.167), kind=kCustom, calls=%fused_computation.clone | custom fusion | bytes 4915320 | tf_op jit(solution)/shard_map/jit(_take)/gather | solution.py:114
  43.9 4.6 %select_bitcast_fusion = (bf16[320,30,128]{2,0,1:T(8,128)(2,1)}, bf16[320,30,128]{2,0,1:T(8,128)(2,1)S(1)}, bf16[320,30,128]{2,0,1:T(8,128)(2,1)S(1)}) fusion(bf16[30,320,128]{2,1,0:T(8,128)(2,1)S(1)} %copy-done.5, pred[30]{0:T(512)(128)(4,1)S(1)} %get-tuple-element.146, bf16[30,320,128]{2,1,0:T(8,128)(2,1)} %gather_fusion.3, ...), kind=kLoop, calls=%fused_computation.37 | loop fusion | flops 3686400 | bytes 14745630 | tf_op jit(solution)/shard_map/jit(_take)/select_n | solution.py:113
  63.2 5.3 %all-to-all-start.1 = ((bf16[16,1,20,10,128]{4,2,3,1,0:T(8,128)(2,1)}), bf16[16,1,20,10,128]{4,2,3,1,0:T(8,128)(2,1)}, u32[]{:S(2)}, u32[]{:S(2)}) async-start(bf16[16,1,20,10,128]{4,2,3,1,0:T(8,128)(2,1)} %fusion.28), calls=%async_computation.1 | async-start | bytes 1966080 | tf_op jit(solution)/shard_map/all_to_all | solution.py:60
  70.5 2.8 %copy.91 = bf16[1,320,10,128]{3,2,0,1:T(8,128)(2,1)} copy(bf16[1,320,10,128]{3,1,2,0:T(8,128)(2,1)} %get-tuple-element.163) | data formatting | bytes 1638400 | tf_op jit(solution)/shard_map/broadcast_in_dim | solution.py:69
  74.1 4.0 %maximum_select_fusion = bf16[640,15,128]{2,0,1:T(8,128)(2,1)} fusion(bf16[320,15,128]{2,0,1:T(8,128)(2,1)} %collective-permute-done, bf16[320,15,128]{2,0,1:T(8,128)(2,1)S(1)} %copy-done.8, pred[]{:T(512)S(6)} %eq.4), kind=kLoop, calls=%fused_computation.33 | loop fusion | flops 11059200 | bytes 4915201 | tf_op jit(solution)/shard_map/jit(_where)/select_n | solution.py:135
  78.1 3.9 %maximum_select_fusion.1 = bf16[640,15,128]{2,0,1:T(8,128)(2,1)} fusion(bf16[320,15,128]{2,0,1:T(8,128)(2,1)} %collective-permute-done.1, bf16[320,15,128]{2,0,1:T(8,128)(2,1)S(1)} %copy-done.9, pred[]{:T(512)S(6)} %eq.4), kind=kLoop, calls=%fused_computation.34 | loop fusion | flops 11059200 | bytes 4915201 | tf_op jit(solution)/shard_map/jit(_where)/select_n | solution.py:135
  82.1 3.8 %maximum_select_fusion.2 = bf16[640,15,128]{2,0,1:T(8,128)(2,1)} fusion(bf16[320,15,128]{2,0,1:T(8,128)(2,1)} %collective-permute-done.2, bf16[320,15,128]{2,0,1:T(8,128)(2,1)S(1)} %copy-done.10, pred[]{:T(512)S(6)} %eq.4), kind=kLoop, calls=%fused_computation.35 | loop fusion | flops 11059200 | bytes 4915201 | tf_op jit(solution)/shard_map/jit(_where)/select_n | solution.py:135
  85.9 6.2 %all-to-all-done.1 = bf16[16,1,20,10,128]{4,2,3,1,0:T(8,128)(2,1)} async-done(((bf16[16,1,20,10,128]{4,2,3,1,0:T(8,128)(2,1)}), bf16[16,1,20,10,128]{4,2,3,1,0:T(8,128)(2,1)}, u32[]{:S(2)}, u32[]{:S(2)}) %all-to-all-start.1) | async-done | bytes 819232 | tf_op jit(solution)/shard_map/all_to_all | solution.py:60
  92.1 4.9 %all-to-all-start = ((bf16[1,320,10,128]{3,2,0,1:T(8,128)(2,1)}), bf16[1,320,10,128]{3,2,0,1:T(8,128)(2,1)S(1)}, u32[]{:S(2)}, u32[]{:S(2)}) async-start(bf16[1,320,10,128]{3,2,0,1:T(8,128)(2,1)} %copy.91), calls=%async_computation | async-start | bytes 2621440 | tf_op jit(solution)/shard_map/all_to_all | solution.py:69
  98.9 50.3 %while.13 = (s32[]{:T(128)}, bf16[640,15,128]{2,0,1:T(8,128)(2,1)}, bf16[640,15,128]{2,0,1:T(8,128)(2,1)}, bf16[640,15,128]{2,0,1:T(8,128)(2,1)}, bf16[640,15,12...) while((s32[]{:T(128)}, bf16[640,15,128]{2,0,1:T(8,128)(2,1)}, ...), condition=%wide.region_5.7_spmd, body=%wide.region_2.6_spmd.sunk | while | flops 1067422080 | bytes 72116400 | solution.py:54
  104.7 8.7 %fusion.66 = bf16[640,5,128]{0,2,1:T(8,128)(2,1)S(1)} fusion(f32[5,640]{1,0:T(8,128)S(1)} %fusion.65, bf16[640,15,128]{2,0,1:T(8,128)(2,1)} %get-tuple-element.219, s32[]{:T(128)S(6)} %select_n.164, f32[5,640,640]{1,2,0:T(8,128)} %copy-done.3), kind=kOutput, calls=%fused_computation.16.clone.1 | convolution fusion | flops 534941440 | bytes 18035204 | tf_op jit(solution)/shard_map/while/body/eval_jaxpr/hrk,khd->rhd/dot_general | solution.py:48
  121.5 8.7 %fusion.66 = bf16[640,5,128]{0,2,1:T(8,128)(2,1)S(1)} fusion(f32[5,640]{1,0:T(8,128)S(1)} %fusion.65, bf16[640,15,128]{2,0,1:T(8,128)(2,1)} %get-tuple-element.219, s32[]{:T(128)S(6)} %select_n.164, f32[5,640,640]{1,2,0:T(8,128)} %copy-done.3), kind=kOutput, calls=%fused_computation.16.clone.1 | convolution fusion | flops 534941440 | bytes 18035204 | tf_op jit(solution)/shard_map/while/body/eval_jaxpr/hrk,khd->rhd/dot_general | solution.py:48
  138.2 8.7 %fusion.66 = bf16[640,5,128]{0,2,1:T(8,128)(2,1)S(1)} fusion(f32[5,640]{1,0:T(8,128)S(1)} %fusion.65, bf16[640,15,128]{2,0,1:T(8,128)(2,1)} %get-tuple-element.219, s32[]{:T(128)S(6)} %select_n.164, f32[5,640,640]{1,2,0:T(8,128)} %copy-done.3), kind=kOutput, calls=%fused_computation.16.clone.1 | convolution fusion | flops 534941440 | bytes 18035204 | tf_op jit(solution)/shard_map/while/body/eval_jaxpr/hrk,khd->rhd/dot_general | solution.py:48
  149.3 4.1 %exponential_reduce_fusion = (f32[2,20,10,8]{3,2,1,0:T(8,128)}, f32[2,20,10,8,8]{3,4,2,1,0:T(8,128)S(1)}) fusion(bf16[8,2,20,10,128]{4,3,2,1,0:T(8,128)(2,1)} %bitcast.30, bf16[8,2,20,10,128]{4,2,3,1,0:T(8,128)(2,1)} %bitcast.27, pred[10,8,8]{1,2,0:T(8,128)(4,1)S(1)} %broadcast_compare_fusion), kind=kOutput, calls=%fused_computation.43 | convolution fusion | flops 6656007 | bytes 1754240 | tf_op jit(solution)/shard_map/sub | solution.py:22
  157.7 6.0 %all-to-all-start.3 = ((bf16[16,20,10,128]{3,1,2,0:T(8,128)(2,1)}), bf16[16,20,10,128]{3,1,2,0:T(8,128)(2,1)}, u32[]{:S(2)}, u32[]{:S(2)}) async-start(bf16[16,20,10,128]{3,1,2,0:T(8,128)(2,1)} %copy.103), calls=%async_computation.3 | async-start | bytes 1966080 | tf_op jit(solution)/shard_map/all_to_all | solution.py:96
  172.2 15.1 %all-to-all-done.3 = bf16[16,20,10,128]{3,1,2,0:T(8,128)(2,1)} async-done(((bf16[16,20,10,128]{3,1,2,0:T(8,128)(2,1)}), bf16[16,20,10,128]{3,1,2,0:T(8,128)(2,1)}, u32[]{:S(2)}, u32[]{:S(2)}) %all-to-all-start.3) | async-done | bytes 819232 | tf_op jit(solution)/shard_map/all_to_all | solution.py:96
  193.0 4.9 %gather_fusion.1 = bf16[40,320,128]{2,1,0:T(8,128)(2,1)} fusion(bf16[320,40,128]{2,0,1:T(8,128)(2,1)} %pad_maximum_fusion, s32[1024]{0:T(1024)S(1)} %pad_clamp_fusion), kind=kCustom, calls=%fused_computation.7 | custom fusion | bytes 6553760 | tf_op jit(solution)/shard_map/jit(_take)/gather | solution.py:152
  197.9 4.3 %bitcast_select_fusion = bf16[320,5120]{1,0:T(8,128)(2,1)} fusion(pred[5120]{0:T(1024)(128)(4,1)S(1)} %broadcast_bitcast_fusion, bf16[40,320,128]{2,1,0:T(8,128)(2,1)} %gather_fusion.1), kind=kLoop, calls=%fused_computation.28 | loop fusion | flops 1638400 | bytes 6558720 | tf_op jit(solution)/shard_map/jit(_take)/select_n | solution.py:152
  (102 shorter events, 76.0 us)
Async XLA Ops:
  0.0 2.9 %copy-start = (bf16[320,5120]{1,0:T(8,128)(2,1)S(1)}, bf16[320,5120]{1,0:T(8,128)(2,1)}, u32[]{:S(2)}) copy-start(bf16[320,5120]{1,0:T(8,128)(2,1)} %param.11) | copy-start | bytes 9830404
  2.9 2.6 %copy-start.12 = (bf16[320,5120]{1,0:T(8,128)(2,1)S(1)}, bf16[320,5120]{1,0:T(8,128)(2,1)}, u32[]{:S(2)}) copy-start(bf16[320,5120]{1,0:T(8,128)(2,1)} %param.12) | copy-start | bytes 9830404
  5.6 2.6 %copy-start.4 = (bf16[320,40,128]{2,0,1:T(8,128)(2,1)S(1)}, bf16[320,40,128]{2,0,1:T(8,128)(2,1)}, u32[]{:S(2)}) copy-start(bf16[320,40,128]{2,0,1:T(8,128)(2,1)} %copy_bitcast_fusion.1) | copy-start | bytes 9830404
  26.3 36.9 %all-to-all-start.2 = ((bf16[1,320,10,128]{3,2,0,1:T(8,128)(2,1)}), bf16[1,320,10,128]{3,2,0,1:T(8,128)(2,1)}, u32[]{:S(2)}, u32[]{:S(2)}) async-start(bf16[1,320,10,128]{3,2,0,1:T(8,128)(2,1)} %copy.96), calls=%async_computation.2 | async-start | bytes 2621440 | tf_op jit(solution)/shard_map/all_to_all | solution.py:68
  39.5 4.4 %copy-start.5 = (bf16[30,320,128]{2,1,0:T(8,128)(2,1)S(1)}, bf16[30,320,128]{2,1,0:T(8,128)(2,1)}, u32[]{:S(2)}) copy-start(bf16[30,320,128]{2,1,0:T(8,128)(2,1)} %gather_fusion.4) | copy-start | bytes 7372804
  50.1 24.0 %collective-permute-start = (bf16[320,15,128]{2,0,1:T(8,128)(2,1)}, bf16[320,15,128]{2,0,1:T(8,128)(2,1)}, u32[]{:S(2)}, u32[]{:S(2)}) collective-permute-start(bf16[320,15,128]{2,0,1:T(8,128)(2,1)} %get-tuple-element.157), channel_id=1, source_target_pairs={{0,1},{1,0},{2,3},{3,2},{4,5},{5,4},{6,7},{7,6},{8,9},{9,8},{10,11... | collective-permute-start | bytes 3686408 | tf_op jit(solution)/shard_map/ppermute | solution.py:17
  50.5 1.8 copy-start.11
  52.1 16.4 %copy-start.6 = (bf16[320,30,128]{2,0,1:T(8,128)(2,1)S(1)}, bf16[320,30,128]{2,0,1:T(8,128)(2,1)}, u32[]{:S(2)}) copy-start(bf16[320,30,128]{2,0,1:T(8,128)(2,1)} %get-tuple-element.158) | copy-start | bytes 7372804
  52.1 26.0 %collective-permute-start.1 = (bf16[320,15,128]{2,0,1:T(8,128)(2,1)}, bf16[320,15,128]{2,0,1:T(8,128)(2,1)}, u32[]{:S(2)}, u32[]{:S(2)}) collective-permute-start(bf16[320,15,128]{2,0,1:T(8,128)(2,1)} %get-tuple-element.155), channel_id=1, source_target_pairs={{0,1},{1,0},{2,3},{3,2},{4,5},{5,4},{6,7},{7,6},{8,9},{9,8},{10,11... | collective-permute-start | bytes 3686408 | tf_op jit(solution)/shard_map/ppermute | solution.py:17
  63.2 28.9 %all-to-all-start.1 = ((bf16[16,1,20,10,128]{4,2,3,1,0:T(8,128)(2,1)}), bf16[16,1,20,10,128]{4,2,3,1,0:T(8,128)(2,1)}, u32[]{:S(2)}, u32[]{:S(2)}) async-start(bf16[16,1,20,10,128]{4,2,3,1,0:T(8,128)(2,1)} %fusion.28), calls=%async_computation.1 | async-start | bytes 1966080 | tf_op jit(solution)/shard_map/all_to_all | solution.py:60
  68.5 4.9 %copy-start.2 = (s32[40]{0:T(128)S(1)}, s32[40]{0:T(128)}, u32[]{:S(2)}) copy-start(s32[40]{0:T(128)} %param.15) | copy-start | bytes 484
  70.1 4.0 %copy-start.8 = (bf16[320,15,128]{2,0,1:T(8,128)(2,1)S(1)}, bf16[320,15,128]{2,0,1:T(8,128)(2,1)}, u32[]{:S(2)}) copy-start(bf16[320,15,128]{2,0,1:T(8,128)(2,1)} %get-tuple-element.156) | copy-start | bytes 3686404
  70.1 12.0 %collective-permute-start.2 = (bf16[320,15,128]{2,0,1:T(8,128)(2,1)}, bf16[320,15,128]{2,0,1:T(8,128)(2,1)}, u32[]{:S(2)}, u32[]{:S(2)}) collective-permute-start(bf16[320,15,128]{2,0,1:T(8,128)(2,1)} %get-tuple-element.153), channel_id=1, source_target_pairs={{0,1},{1,0},{2,3},{3,2},{4,5},{5,4},{6,7},{7,6},{8,9},{9,8},{10,11... | collective-permute-start | bytes 3686408 | tf_op jit(solution)/shard_map/ppermute | solution.py:17
  74.1 4.0 %copy-start.9 = (bf16[320,15,128]{2,0,1:T(8,128)(2,1)S(1)}, bf16[320,15,128]{2,0,1:T(8,128)(2,1)}, u32[]{:S(2)}) copy-start(bf16[320,15,128]{2,0,1:T(8,128)(2,1)} %get-tuple-element.154) | copy-start | bytes 3686404
  78.1 4.0 %copy-start.10 = (bf16[320,15,128]{2,0,1:T(8,128)(2,1)S(1)}, bf16[320,15,128]{2,0,1:T(8,128)(2,1)}, u32[]{:S(2)}) copy-start(bf16[320,15,128]{2,0,1:T(8,128)(2,1)} %get-tuple-element.152) | copy-start | bytes 3686404
  92.1 61.3 %all-to-all-start = ((bf16[1,320,10,128]{3,2,0,1:T(8,128)(2,1)}), bf16[1,320,10,128]{3,2,0,1:T(8,128)(2,1)S(1)}, u32[]{:S(2)}, u32[]{:S(2)}) async-start(bf16[1,320,10,128]{3,2,0,1:T(8,128)(2,1)} %copy.91), calls=%async_computation | async-start | bytes 2621440 | tf_op jit(solution)/shard_map/all_to_all | solution.py:69
  101.5 3.2 %copy-start.3 = (f32[5,640,640]{1,2,0:T(8,128)}, f32[5,640,640]{1,2,0:T(8,128)S(1)}, u32[]{:S(2)}) copy-start(f32[5,640,640]{1,2,0:T(8,128)S(1)} %fusion.64) | copy-start | bytes 24576004 | tf_op jit(solution)/shard_map/while
  118.3 3.2 %copy-start.3 = (f32[5,640,640]{1,2,0:T(8,128)}, f32[5,640,640]{1,2,0:T(8,128)S(1)}, u32[]{:S(2)}) copy-start(f32[5,640,640]{1,2,0:T(8,128)S(1)} %fusion.64) | copy-start | bytes 24576004 | tf_op jit(solution)/shard_map/while
  135.1 3.2 %copy-start.3 = (f32[5,640,640]{1,2,0:T(8,128)}, f32[5,640,640]{1,2,0:T(8,128)S(1)}, u32[]{:S(2)}) copy-start(f32[5,640,640]{1,2,0:T(8,128)S(1)} %fusion.64) | copy-start | bytes 24576004 | tf_op jit(solution)/shard_map/while
  155.2 8.6 %copy-start.7 = (bf16[640,15,128]{2,0,1:T(8,128)(2,1)S(1)}, bf16[640,15,128]{2,0,1:T(8,128)(2,1)}, u32[]{:S(2)}) copy-start(bf16[640,15,128]{2,0,1:T(8,128)(2,1)} %get-tuple-element.105) | copy-start | bytes 7372804
  157.7 29.6 %all-to-all-start.3 = ((bf16[16,20,10,128]{3,1,2,0:T(8,128)(2,1)}), bf16[16,20,10,128]{3,1,2,0:T(8,128)(2,1)}, u32[]{:S(2)}, u32[]{:S(2)}) async-start(bf16[16,20,10,128]{3,1,2,0:T(8,128)(2,1)} %copy.103), calls=%async_computation.3 | async-start | bytes 1966080 | tf_op jit(solution)/shard_map/all_to_all | solution.py:96
  165.4 3.1 %collective-permute-start.3 = (bf16[320,15,128]{2,0,1:T(8,128)(2,1)}, bf16[320,15,128]{2,0,1:T(8,128)(2,1)S(1)}, u32[]{:S(2)}, u32[]{:S(2)}) collective-permute-start(bf16[320,15,128]{2,0,1:T(8,128)(2,1)} %get-tuple-element.151), channel_id=1, source_target_pairs={{0,1},{1,0},{2,3},{3,2},{4,5},{5,4},{6,7},{7,6},{8,9},{9,8},{10,11... | collective-permute-start | bytes 3686408 | tf_op jit(solution)/shard_map/ppermute | solution.py:17
  168.5 1.0 copy-start.13
  193.0 9.2 %copy-start.1 = (bf16[320,5120]{1,0:T(8,128)(2,1)S(1)}, bf16[320,5120]{1,0:T(8,128)(2,1)}, u32[]{:S(2)}) copy-start(bf16[320,5120]{1,0:T(8,128)(2,1)} %param.11) | copy-start | bytes 9830404
